TPU v7x, 32 devices: a whole 2x2x4 slice. The times are simulated.
32 devices in a mesh: energy: 8 (over y, x, core), slab: 4 (over z).
Axes of the slice: x: 2, y: 2, z: 4, core: 2. Of those that a mesh axis runs over, the one named last changes fastest.
Arguments:
- hamiltonian: float32 [4, 2, 256, 256], P('slab'), may hold values from -1 to 1, as said below
- contact: float32 [2, 8, 2, 2, 256, 256], P(None, 'energy'), may hold values from -0.109375 to 0.109375
- hop: float32 [3, 256], replicated, may hold values from 0.4 to 1.2
- bond: int32 [3, 256], replicated, may hold values from 0 to 255, each once within a row
- shifts: int32 [4], replicated, may hold values from -3 to 3, as said below
- strength: float32 [4], replicated, may hold values from 0.1 to 0.4
- coupling: float32 [256, 256], replicated, may hold values from -0.375 to 0.375
Outputs:
- green: float32 [2, 8, 4, 2, 256, 256], P(None, 'energy', 'slab')
- self_energy: float32 [2, 8, 4, 2, 256, 256], P(None, 'energy', 'slab')
- density: float32 [4, 256], P('slab')
Inputs may be any that keep to these rules, and one draw needn't show every extreme that they name: `hamiltonian`: each slab's block is Hermitian: the real part symmetric, the imaginary part antisymmetric with a zero diagonal. `shifts`: the table is 3, -3, k, -k in this order, for some k with 1 <= k < 3.
All inputs are finite; a program needn't handle non-finite values.
Results may differ from a plain program's by a relative error of at most 0.0001.
Values sent between devices are 32-bit elements; how exact they have to be, the bound alone decides.
A program may use at most 128 MiB of HBM per device.

v0:
```python
import functools
import math

import jax
import jax.numpy as jnp
from jax import lax
from jax.experimental import pallas as pl
from jax.experimental.pallas import tpu as pltpu
from jax.sharding import PartitionSpec as P

KMAX = 3
BROADENING = 0.5
ENERGY_LOW = 4.0
ENERGY_SPAN = 1.0
MESH = pl.DeviceIdType.MESH
VMEM_LIMIT = 56 * 1024 * 1024
F32 = jnp.float32
BF16 = jnp.bfloat16


def iotas(shape):
    return (
        lax.broadcasted_iota(jnp.int32, shape, 0),
        lax.broadcasted_iota(jnp.int32, shape, 1),
    )


def split(x):
    high = x.astype(BF16)
    return high, (x - high.astype(F32)).astype(BF16)


def dot(a, b):
    return jnp.dot(a, b, preferred_element_type=F32)


def product(a, b):
    size = a[0].shape[-1]
    ar, al = split(a[0])
    ai, am = split(a[1])
    br, bl = split(b[0])
    bi, bm = split(b[1])
    left = jnp.concatenate([ar, al, ar, ai, am, ai], axis=1)
    real = jnp.concatenate([br, br, bl, -bi, -bi, -bm], axis=0)
    imag = jnp.concatenate([bi, bi, bm, br, br, bl], axis=0)
    return dot(left, real), dot(left, imag)


def invert(x):
    size = x[0].shape[-1]
    rows, cols = iotas((size, size))
    eye = rows == cols
    out = []
    recips = []
    for axis in (0, 1):
        dr = jnp.sum(jnp.where(eye, x[0], 0.0), axis=axis, keepdims=True)
        di = jnp.sum(jnp.where(eye, x[1], 0.0), axis=axis, keepdims=True)
        modulus = dr * dr + di * di
        recips.append((dr / modulus, -di / modulus))
    (cr, ci), (rr, ri) = recips
    pr = x[0] * cr - x[1] * ci
    pi = x[0] * ci + x[1] * cr
    qr = jnp.where(eye, 2.0, 0.0) - pr
    qi = -pi
    first = (rr * qr - ri * qi, rr * qi + ri * qr)
    yr, yi = product(x, first)
    return product(first, (jnp.where(eye, 2.0, 0.0) - yr, -yi))


def conjugate(x, coupler):
    left, right, scale_col, scale_row = coupler
    size = left.shape[0]
    hr, lr = split(x[0])
    hi, li = split(x[1])
    moved = dot(left, jnp.concatenate([hr, hi, lr, li], axis=1)).astype(BF16)
    stacked = jnp.concatenate([moved[:, i * size : (i + 1) * size] for i in range(4)], axis=0)
    full = dot(stacked, right)
    real = (full[:size] + full[2 * size : 3 * size]) * scale_col * scale_row
    imag = (full[size : 2 * size] + full[3 * size :]) * scale_col * scale_row
    return real, imag


def gather_kernel(slabs, columns, ham_ref, hall_ref, send1, recv1, send2, recv2):
    column = lax.axis_index("energy")
    slab = lax.axis_index("slab")
    size = ham_ref.shape[-1]
    depth = size // columns
    rows, cols = iotas((size, size))

    barrier = pltpu.get_barrier_semaphore()
    for dz in range(1, slabs):
        pl.semaphore_signal(
            barrier, inc=1, device_id=(column, lax.rem(slab + dz, slabs)), device_id_type=MESH
        )
    for dc in range(1, columns):
        pl.semaphore_signal(
            barrier, inc=1, device_id=(lax.rem(column + dc, columns), slab), device_id_type=MESH
        )
    hall_ref[slab] = jnp.where(rows <= cols, ham_ref[0], ham_ref[1])
    pl.semaphore_wait(barrier, slabs - 1 + columns - 1)

    own = pl.ds(pl.multiple_of(column * depth, depth), depth)

    def along(dz):
        return pltpu.make_async_remote_copy(
            src_ref=hall_ref.at[slab, own],
            dst_ref=hall_ref.at[slab, own],
            send_sem=send1.at[dz],
            recv_sem=recv1.at[dz],
            device_id=(column, lax.rem(slab + dz, slabs)),
            device_id_type=MESH,
        )

    def arrived_along(dz):
        source = lax.rem(slab - dz + slabs, slabs)
        return pltpu.make_async_remote_copy(
            src_ref=hall_ref.at[source, own],
            dst_ref=hall_ref.at[source, own],
            send_sem=send1.at[dz],
            recv_sem=recv1.at[dz],
            device_id=(column, source),
            device_id_type=MESH,
        )

    def across(dz, dc):
        source = lax.rem(slab - dz + slabs, slabs)
        return pltpu.make_async_remote_copy(
            src_ref=hall_ref.at[source, own],
            dst_ref=hall_ref.at[source, own],
            send_sem=send2.at[dz, dc],
            recv_sem=recv2.at[dz, dc],
            device_id=(lax.rem(column + dc, columns), slab),
            device_id_type=MESH,
        )

    def arrived_across(dz, dc):
        source = lax.rem(slab - dz + slabs, slabs)
        partner = lax.rem(column - dc + columns, columns)
        theirs = pl.ds(pl.multiple_of(partner * depth, depth), depth)
        return pltpu.make_async_remote_copy(
            src_ref=hall_ref.at[source, theirs],
            dst_ref=hall_ref.at[source, theirs],
            send_sem=send2.at[dz, dc],
            recv_sem=recv2.at[dz, dc],
            device_id=(partner, slab),
            device_id_type=MESH,
        )

    for dz in range(1, slabs):
        along(dz).start()
    for dz in range(1, slabs):
        arrived_along(dz).wait_recv()
        for dc in range(1, columns):
            across(dz, dc).start()
    for dz in range(1, slabs):
        for dc in range(1, columns):
            arrived_across(dz, dc).wait_recv()
    for dz in range(1, slabs):
        along(dz).wait_send()
        for dc in range(1, columns):
            across(dz, dc).wait_send()


def chain_kernel(slabs, columns, hall_ref, contact_ref, hop_ref, bond_ref, green_ref):
    column = lax.axis_index("energy")
    slab = lax.axis_index("slab")
    row_count = contact_ref.shape[0]
    size = hall_ref.shape[-1]
    half = slabs // 2
    is_left = slab < half
    rows, cols = iotas((size, size))
    eye = rows == cols

    def choose(left, right):
        return jnp.where(is_left, left, right)

    def coupler(k, down):
        bond = bond_ref[pl.ds(k, 1), :]
        hop_row = hop_ref[pl.ds(k, 1), :]
        hop_col = jnp.sum(jnp.where(eye, hop_row, 0.0), axis=1, keepdims=True)
        turned = jnp.where(rows == bond, 1.0, 0.0).astype(F32)
        plain = turned.T
        moved_col = jnp.sum(turned * hop_row, axis=1, keepdims=True)
        moved_row = jnp.sum(plain * hop_col, axis=0, keepdims=True)
        up = (plain.astype(BF16), turned.astype(BF16), hop_col, hop_row)
        lower = (turned.astype(BF16), plain.astype(BF16), moved_col, moved_row)
        flag = down.astype(F32)
        inner = [
            (flag * d.astype(F32) + (1.0 - flag) * u.astype(F32)).astype(u.dtype)
            for d, u in zip(lower[:2], up[:2])
        ]
        scales = [jnp.where(down, d, u) for d, u in zip(lower[2:], up[2:])]
        reverse = [jnp.where(down, u, d) for d, u in zip(lower[2:], up[2:])]
        return tuple(inner + scales), tuple(inner[::-1] + reverse)

    def onsite(index):
        packed = hall_ref[index]
        turned = packed.T
        real = jnp.where(rows <= cols, packed, turned)
        imag = jnp.where(rows > cols, packed, jnp.where(rows < cols, -turned, 0.0))
        return real, imag

    last = slabs - 1
    near_index, far_index = choose(0, last), choose(last, 0)
    near_ham, far_ham = onsite(near_index), onsite(far_index)
    mid_ham = onsite(choose(half - 1, half))
    cross_ham = onsite(choose(half, half - 1))
    near_side, near_back = coupler(choose(0, last - 1), is_left)
    far_side, _ = coupler(choose(last - 1, 0), jnp.logical_not(is_left))
    cross_side, _ = coupler(half - 1, jnp.logical_not(is_left))

    def base(r, ham):
        position = (r * columns + column).astype(F32)
        energy = ENERGY_LOW + ENERGY_SPAN * position / (row_count * columns)
        return (
            jnp.where(eye, energy, 0.0) - ham[0],
            jnp.where(eye, BROADENING, 0.0) - ham[1],
        )

    def minus(a, b):
        return a[0] - b[0], a[1] - b[1]

    span = range(row_count)
    near_end, far_end = choose(0, 1), choose(1, 0)
    near = [
        invert(minus(base(r, near_ham), (contact_ref[r, near_end, 0], contact_ref[r, near_end, 1])))
        for r in span
    ]
    far = [
        invert(minus(base(r, far_ham), (contact_ref[r, far_end, 0], contact_ref[r, far_end, 1])))
        for r in span
    ]
    reduced = [minus(base(r, mid_ham), conjugate(near[r], near_side)) for r in span]
    opposite = [invert(minus(base(r, cross_ham), conjugate(far[r], far_side))) for r in span]
    green = [invert(minus(reduced[r], conjugate(opposite[r], cross_side))) for r in span]
    for r in span:
        green_ref[r, 0] = green[r][0]
        green_ref[r, 1] = green[r][1]

    @pl.when(jnp.logical_or(slab == 0, slab == last))
    def _():
        for r in span:
            inner = conjugate((green_ref[r, 0], green_ref[r, 1]), near_back)
            change = product(product(near[r], inner), near[r])
            green_ref[r, 0] = near[r][0] + change[0]
            green_ref[r, 1] = near[r][1] + change[1]


def phonon_kernel(
    columns, shifts_ref, strength_ref, green_ref, summed_ref, density_ref,
    taken, mixed, shares, send1, recv1, send2, recv2, send3, recv3,
):
    column = lax.axis_index("energy")
    slab = lax.axis_index("slab")
    row_count = green_ref.shape[0]
    size = green_ref.shape[-1]
    depth = size // columns
    count = row_count * columns

    def partner(dc):
        return lax.rem(column + dc + columns, columns)

    def part(index):
        return pl.ds(pl.multiple_of(index * depth, depth), depth)

    barrier = pltpu.get_barrier_semaphore()
    for dc in range(1, columns):
        pl.semaphore_signal(barrier, inc=1, device_id=(partner(dc), slab), device_id_type=MESH)
    taken[:, column] = green_ref[:, :, part(column), :]
    pl.semaphore_wait(barrier, columns - 1)

    def copy(source, target, send, recv, dc, other):
        return pltpu.make_async_remote_copy(
            src_ref=source, dst_ref=target, send_sem=send.at[dc], recv_sem=recv.at[dc],
            device_id=(other, slab), device_id_type=MESH,
        )

    def outward(dc):
        other = partner(dc)
        return copy(
            green_ref.at[:, :, part(other), :], taken.at[:, column], send1, recv1, dc, other
        )

    def outward_in(dc):
        other = partner(-dc)
        return copy(
            green_ref.at[:, :, part(other), :], taken.at[:, other], send1, recv1, dc, other
        )

    def homeward(dc):
        other = partner(dc)
        return copy(
            mixed.at[:, other], summed_ref.at[:, :, part(column), :], send2, recv2, dc, other
        )

    def homeward_in(dc):
        other = partner(-dc)
        return copy(
            mixed.at[:, other], summed_ref.at[:, :, part(other), :], send2, recv2, dc, other
        )

    def share(dc):
        return copy(shares.at[column], shares.at[column], send3, recv3, dc, partner(dc))

    def share_in(dc):
        other = partner(-dc)
        return copy(shares.at[other], shares.at[other], send3, recv3, dc, other)

    others = range(1, columns)
    for dc in others:
        outward(dc).start()
    weights = {}
    for d in range(-KMAX, KMAX + 1):
        if d != 0:
            weights[d] = sum(
                jnp.where(shifts_ref[m] == d, strength_ref[m], 0.0)
                for m in range(shifts_ref.shape[0])
            )
    for dc in others:
        outward_in(dc).wait_recv()

    for e in range(count):
        r, c = divmod(e, columns)
        total = None
        for d, weight in weights.items():
            if 0 <= e + d < count:
                term = weight * taken[(e + d) // columns, (e + d) % columns]
                total = term if total is None else total + term
        mixed[r, c] = total
    for dc in others:
        homeward(dc).start()

    levels = jnp.zeros((depth, size), F32)
    for e in range(count):
        energy = ENERGY_LOW + ENERGY_SPAN * e / count
        occupation = 1.0 / (1.0 + math.exp(3.0 * (energy - (ENERGY_LOW + 0.5 * ENERGY_SPAN))))
        levels = levels - occupation * taken[e // columns, e % columns, 1]
    local_rows, local_cols = iotas((depth, size))
    diagonal = jnp.where(local_rows + column * depth == local_cols, levels, 0.0)
    own_share = jnp.sum(diagonal, axis=0, keepdims=True)
    shares[column] = jnp.broadcast_to(own_share, (8, size))
    for dc in others:
        share(dc).start()

    summed_ref[:, :, part(column), :] = mixed[:, column]
    for dc in others:
        share_in(dc).wait_recv()
    density_ref[...] = jnp.sum(shares[...], axis=0)[:1]
    for dc in others:
        homeward_in(dc).wait_recv()
    for dc in others:
        outward(dc).wait_send()
        homeward(dc).wait_send()
        share(dc).wait_send()


def coupling_kernel(summed_ref, coupling_ref, out_ref):
    size = coupling_ref.shape[0]
    high, low = split(coupling_ref[...])
    left = jnp.concatenate([high, low, high], axis=1)
    right_high, right_low = split(coupling_ref[...].T)
    right = jnp.concatenate([right_high, right_high, right_low], axis=0)
    for r in range(summed_ref.shape[0]):
        for part in range(2):
            a, b = split(summed_ref[r, part])
            half = dot(left, jnp.concatenate([a, a, b], axis=0))
            a, b = split(half)
            out_ref[r, part] = dot(jnp.concatenate([a, b, a], axis=1), right)


def whole():
    return pl.BlockSpec(memory_space=pltpu.VMEM)


def scalar():
    return pl.BlockSpec(memory_space=pltpu.SMEM)


def per_device(slabs, columns, hamiltonian, contact, hop, bond, shifts, strength, coupling):
    size = hamiltonian.shape[-1]
    row_count = contact.shape[0]
    depth = size // columns
    dma = pltpu.SemaphoreType.DMA
    hall = pl.pallas_call(
        functools.partial(gather_kernel, slabs, columns),
        out_shape=jax.ShapeDtypeStruct((slabs, size, size), F32),
        in_specs=[whole()],
        out_specs=whole(),
        scratch_shapes=[
            dma((slabs,)), dma((slabs,)), dma((slabs, columns)), dma((slabs, columns))
        ],
        compiler_params=pltpu.CompilerParams(
            collective_id=0, has_side_effects=True, vmem_limit_bytes=VMEM_LIMIT
        ),
        name="gather_hamiltonian",
    )(hamiltonian[0])
    block = jax.ShapeDtypeStruct((row_count, 2, size, size), F32)
    green = pl.pallas_call(
        functools.partial(chain_kernel, slabs, columns),
        out_shape=block,
        in_specs=[whole()] * 4,
        out_specs=whole(),
        compiler_params=pltpu.CompilerParams(vmem_limit_bytes=VMEM_LIMIT),
        name="chain",
    )(hall, contact[:, 0], hop, bond)
    table = pltpu.VMEM((row_count, columns, 2, depth, size), F32)
    summed, density = pl.pallas_call(
        functools.partial(phonon_kernel, columns),
        out_shape=(block, jax.ShapeDtypeStruct((1, size), F32)),
        in_specs=[scalar(), scalar(), whole()],
        out_specs=(whole(), whole()),
        scratch_shapes=[table, table, pltpu.VMEM((columns, 8, size), F32)]
        + [dma((columns,))] * 6,
        compiler_params=pltpu.CompilerParams(
            collective_id=1, has_side_effects=True, vmem_limit_bytes=VMEM_LIMIT
        ),
        name="phonon_sum",
    )(shifts, strength, green)
    self_energy = pl.pallas_call(
        coupling_kernel,
        out_shape=block,
        in_specs=[whole()] * 2,
        out_specs=whole(),
        compiler_params=pltpu.CompilerParams(vmem_limit_bytes=VMEM_LIMIT),
        name="coupling",
    )(summed, coupling)
    return (green[:, None, None], self_energy[:, None, None], density)


def solution(mesh):
    in_specs = (
        P("slab", None, None, None),
        P(None, "energy", None, None, None, None),
        P(),
        P(),
        P(),
        P(),
        P(),
    )
    out_specs = (
        P(None, "energy", "slab", None, None, None),
        P(None, "energy", "slab", None, None, None),
        P("slab", None),
    )
    return jax.shard_map(
        functools.partial(per_device, mesh.shape["slab"], mesh.shape["energy"]),
        mesh=mesh, in_specs=in_specs, out_specs=out_specs, check_vma=False,
    )
```

profile of v0, /device:TPU:0, one launch (start us, length us, event | category | flops | bytes accessed | tf_op | source)
XLA Modules:
  0.0 75.2 jit_solution(238229722417586202)
XLA Ops:
  0.6 21.1 %gather_hamiltonian.1.hall_ref = f32[4,256,256]{2,1,0:T(8,128)} custom-call(f32[2,256,256]{2,1,0:T(8,128)} %bitcast.11), custom_call_target="tpu_custom_call" | custom-call | tf_op jit(solution)/shard_map/gather_hamiltonian/pallas_call | solution.py:384
  21.7 18.0 %chain.1.green_ref = f32[2,2,256,256]{3,2,1,0:T(8,128)} custom-call(f32[4,256,256]{2,1,0:T(8,128)} %gather_hamiltonian.1.hall_ref, f32[2,2,2,256,256]{4,3,2,1,0:T(8,128)} %bitcast.9, f32[3,256]{1,0:T(4,128)} %hop_ref.1, s32[3,256]{1,0:T(4,128)} %bond_ref.1), custom_call_target="tpu_custom_call" | custom-call | tf_op jit(solution)/shard_map/chain/pallas_call | solution.py:398
  39.7 31.4 %phonon_sum.1 = (f32[2,2,256,256]{3,2,1,0:T(8,128)}, f32[1,256]{1,0:T(1,128)}) custom-call(s32[4]{0:T(128)} %shifts_ref.1, f32[4]{0:T(128)} %strength_ref.1, f32[2,2,256,256]{3,2,1,0:T(8,128)} %chain.1.green_ref), custom_call_target="tpu_custom_call" | custom-call | tf_op jit(solution)/shard_map/phonon_sum/pallas_call | solution.py:407
  71.1 0.0 copy-start
  71.1 3.5 %coupling.1 = f32[2,2,256,256]{3,2,1,0:T(8,128)} custom-call(f32[2,2,256,256]{3,2,1,0:T(8,128)} %get-tuple-element.5.summed_ref, f32[256,256]{1,0:T(8,128)} %coupling_ref.1), custom_call_target="tpu_custom_call" | custom-call | tf_op jit(solution)/shard_map/coupling/pallas_call | solution.py:419
  74.6 0.0 copy-done
  74.6 0.6 copy.13
Async XLA Ops:
  71.1 3.5 %copy-start = (f32[1,256]{1,0:T(1,128)S(1)}, f32[1,256]{1,0:T(1,128)}, u32[]{:S(2)}) copy-start(f32[1,256]{1,0:T(1,128)} %get-tuple-element.15) | copy-start | bytes 3076
where the time goes:
time: 75.4 us; the launch traced here: 75.2 us
  Pallas kernels  73.9 us (98%)
    pallas_call x1, Pallas kernels, per_device(): pl.pallas_call(functools.partial(phonon_kernel, columns), out_shape=(bloc...  31.4 us
    pallas_call x1, Pallas kernels, per_device(): pl.pallas_call(functools.partial(gather_kernel, slabs, columns), out_shap...  21.1 us
    pallas_call x1, Pallas kernels, per_device(): pl.pallas_call(functools.partial(chain_kernel, slabs, columns), out_shape...  18 us
    pallas_call x1, Pallas kernels, per_device(): pl.pallas_call(coupling_kernel, out_shape=block, in_specs=[whole()] * 2,...  3.46 us

commit v1 on v0

v1 whole, which is shorter than its diff:
```python
import functools
import math

import jax
import jax.numpy as jnp
from jax import lax
from jax.experimental import pallas as pl
from jax.experimental.pallas import tpu as pltpu
from jax.sharding import PartitionSpec as P

KMAX = 3
BROADENING = 0.5
ENERGY_LOW = 4.0
ENERGY_SPAN = 1.0
MESH = pl.DeviceIdType.MESH
VMEM_LIMIT = 56 * 1024 * 1024
F32 = jnp.float32
BF16 = jnp.bfloat16


def iotas(shape):
    return (
        lax.broadcasted_iota(jnp.int32, shape, 0),
        lax.broadcasted_iota(jnp.int32, shape, 1),
    )


def split(x):
    high = x.astype(BF16)
    return high, (x - high.astype(F32)).astype(BF16)


def dot(a, b):
    return jnp.dot(a, b, preferred_element_type=F32)


def product(a, b):
    size = a[0].shape[-1]
    ar, al = split(a[0])
    ai, am = split(a[1])
    br, bl = split(b[0])
    bi, bm = split(b[1])
    left = jnp.concatenate([ar, al, ar, ai, am, ai], axis=1)
    real = jnp.concatenate([br, br, bl, -bi, -bi, -bm], axis=0)
    imag = jnp.concatenate([bi, bi, bm, br, br, bl], axis=0)
    return dot(left, real), dot(left, imag)


def invert(x):
    size = x[0].shape[-1]
    rows, cols = iotas((size, size))
    eye = rows == cols
    out = []
    recips = []
    for axis in (0, 1):
        dr = jnp.sum(jnp.where(eye, x[0], 0.0), axis=axis, keepdims=True)
        di = jnp.sum(jnp.where(eye, x[1], 0.0), axis=axis, keepdims=True)
        modulus = dr * dr + di * di
        recips.append((dr / modulus, -di / modulus))
    (cr, ci), (rr, ri) = recips
    pr = x[0] * cr - x[1] * ci
    pi = x[0] * ci + x[1] * cr
    qr = jnp.where(eye, 2.0, 0.0) - pr
    qi = -pi
    first = (rr * qr - ri * qi, rr * qi + ri * qr)
    yr, yi = product(x, first)
    return product(first, (jnp.where(eye, 2.0, 0.0) - yr, -yi))


def conjugate(x, coupler):
    left, right, scale_col, scale_row = coupler
    size = left.shape[0]
    hr, lr = split(x[0])
    hi, li = split(x[1])
    moved = dot(left, jnp.concatenate([hr, hi, lr, li], axis=1)).astype(BF16)
    stacked = jnp.concatenate([moved[:, i * size : (i + 1) * size] for i in range(4)], axis=0)
    full = dot(stacked, right)
    real = (full[:size] + full[2 * size : 3 * size]) * scale_col * scale_row
    imag = (full[size : 2 * size] + full[3 * size :]) * scale_col * scale_row
    return real, imag


def born_kernel(
    slabs, columns, ham_ref, contact_ref, hop_ref, bond_ref, shifts_ref, strength_ref,
    coupling_ref, green_ref, summed_ref, density_ref, hall, taken, mixed, shares,
    send_z, recv_z, send_h, recv_h, send1, recv1, send2, recv2, send3, recv3,
):
    column = lax.axis_index("energy")
    slab = lax.axis_index("slab")
    row_count = contact_ref.shape[0]
    size = ham_ref.shape[-1]
    depth = size // columns
    count = row_count * columns
    half = slabs // 2
    last = slabs - 1
    span = range(row_count)
    others = range(1, columns)
    is_left = slab < half
    rows, cols = iotas((size, size))
    eye = rows == cols

    def partner(dc):
        return lax.rem(column + dc + columns, columns)

    def part(index):
        return pl.ds(pl.multiple_of(index * depth, depth), depth)

    def copy(source, target, send, recv, device):
        return pltpu.make_async_remote_copy(
            src_ref=source, dst_ref=target, send_sem=send, recv_sem=recv,
            device_id=device, device_id_type=MESH,
        )

    barrier = pltpu.get_barrier_semaphore()
    for dz in range(1, slabs):
        pl.semaphore_signal(
            barrier, inc=1, device_id=(column, lax.rem(slab + dz, slabs)), device_id_type=MESH
        )
    for dc in others:
        pl.semaphore_signal(barrier, inc=1, device_id=(partner(dc), slab), device_id_type=MESH)
    hall[slab] = jnp.where(rows <= cols, ham_ref[0], ham_ref[1])
    pl.semaphore_wait(barrier, slabs - 1 + columns - 1)

    def along(target):
        piece = hall.at[slab, part(column)]
        return copy(piece, piece, send_z.at[target], recv_z.at[slab], (column, target))

    def along_in(source):
        piece = hall.at[source, part(column)]
        return copy(piece, piece, send_z.at[source], recv_z.at[source], (column, source))

    def across(source, dc):
        piece = hall.at[source, part(column)]
        return copy(
            piece, piece, send_h.at[source, dc], recv_h.at[source, dc], (partner(dc), slab)
        )

    def across_in(source, dc):
        other = partner(-dc)
        piece = hall.at[source, part(other)]
        return copy(piece, piece, send_h.at[source, dc], recv_h.at[source, dc], (other, slab))

    for target in range(slabs):
        @pl.when(slab != target)
        def _():
            along(target).start()

    def choose(left, right):
        return jnp.where(is_left, left, right)

    def coupler(k, down):
        bond = bond_ref[pl.ds(k, 1), :]
        hop_row = hop_ref[pl.ds(k, 1), :]
        hop_col = jnp.sum(jnp.where(eye, hop_row, 0.0), axis=1, keepdims=True)
        turned = jnp.where(rows == bond, 1.0, 0.0).astype(F32)
        plain = turned.T
        moved_col = jnp.sum(turned * hop_row, axis=1, keepdims=True)
        moved_row = jnp.sum(plain * hop_col, axis=0, keepdims=True)
        flag = down.astype(F32)
        left = (flag * turned + (1.0 - flag) * plain).astype(BF16)
        right = (flag * plain + (1.0 - flag) * turned).astype(BF16)
        scales = (jnp.where(down, moved_col, hop_col), jnp.where(down, moved_row, hop_row))
        reverse = (jnp.where(down, hop_col, moved_col), jnp.where(down, hop_row, moved_row))
        return (left, right) + scales, (right, left) + reverse

    near_side, near_back = coupler(choose(0, last - 1), is_left)
    far_side, _ = coupler(choose(last - 1, 0), jnp.logical_not(is_left))
    cross_side, _ = coupler(half - 1, jnp.logical_not(is_left))

    order = [0, last] + list(range(1, last))
    for source in order:
        @pl.when(slab != source)
        def _():
            along_in(source).wait_recv()
            for dc in others:
                across(source, dc).start()

    def arrive(source, wanted):
        @pl.when(jnp.logical_and(slab != source, wanted))
        def _():
            for dc in others:
                across_in(source, dc).wait_recv()

    def onsite(index):
        packed = hall[index]
        turned = packed.T
        real = jnp.where(rows <= cols, packed, turned)
        imag = jnp.where(rows > cols, packed, jnp.where(rows < cols, -turned, 0.0))
        return real, imag

    def base(r, ham):
        position = (r * columns + column).astype(F32)
        energy = ENERGY_LOW + ENERGY_SPAN * position / count
        return (
            jnp.where(eye, energy, 0.0) - ham[0],
            jnp.where(eye, BROADENING, 0.0) - ham[1],
        )

    def minus(a, b):
        return a[0] - b[0], a[1] - b[1]

    def end_inverses(index, end):
        ham = onsite(index)
        return [
            invert(minus(base(r, ham), (contact_ref[r, end, 0], contact_ref[r, end, 1])))
            for r in span
        ]

    is_right = jnp.logical_not(is_left)
    arrive(0, is_left)
    arrive(last, is_right)
    near = end_inverses(choose(0, last), choose(0, 1))
    arrive(0, is_right)
    arrive(last, is_left)
    far = end_inverses(choose(last, 0), choose(1, 0))
    for source in range(1, last):
        arrive(source, slab >= 0)
    mid_ham = onsite(choose(half - 1, half))
    cross_ham = onsite(choose(half, half - 1))

    def outward(r, dc):
        other = partner(dc)
        return copy(
            green_ref.at[r, :, part(other), :], taken.at[r * columns + column],
            send1.at[r, dc], recv1.at[r, dc], (other, slab),
        )

    def outward_in(r, dc):
        other = partner(-dc)
        return copy(
            green_ref.at[r, :, part(other), :], taken.at[r * columns + other],
            send1.at[r, dc], recv1.at[r, dc], (other, slab),
        )

    for r in span:
        opposite = invert(minus(base(r, cross_ham), conjugate(far[r], far_side)))
        reduced = minus(base(r, mid_ham), conjugate(near[r], near_side))
        middle = invert(minus(reduced, conjugate(opposite, cross_side)))
        green_ref[r, 0] = middle[0]
        green_ref[r, 1] = middle[1]

        @pl.when(jnp.logical_or(slab == 0, slab == last))
        def _():
            inner = conjugate((green_ref[r, 0], green_ref[r, 1]), near_back)
            change = product(product(near[r], inner), near[r])
            green_ref[r, 0] = near[r][0] + change[0]
            green_ref[r, 1] = near[r][1] + change[1]

        for dc in others:
            outward(r, dc).start()
        taken[r * columns + column] = green_ref[r, :, part(column), :]

    weights = {}
    for d in range(-KMAX, KMAX + 1):
        if d != 0:
            weights[d] = sum(
                jnp.where(shifts_ref[m] == d, strength_ref[m], 0.0)
                for m in range(shifts_ref.shape[0])
            )
    high, low = split(coupling_ref[...].T)
    right = jnp.concatenate([high, high, low], axis=0)

    def mix(target):
        pieces = []
        for r in span:
            place = r * columns + target
            total = jnp.zeros((2, depth, size), F32)
            for d, weight in weights.items():
                inside = jnp.logical_and(place + d >= 0, place + d < count)
                index = jnp.clip(place + d, 0, count - 1)
                total = total + jnp.where(inside, weight, 0.0) * taken[index]
            pieces.append(total.reshape(2 * depth, size))
        a, b = split(jnp.concatenate(pieces, axis=0))
        moved = dot(jnp.concatenate([a, b, a], axis=1), right)
        return moved.reshape(row_count, 2, depth, size)

    def homeward(dc):
        return copy(
            mixed.at[dc], summed_ref.at[:, :, part(column), :],
            send2.at[dc], recv2.at[dc], (partner(dc), slab),
        )

    def homeward_in(dc):
        other = partner(-dc)
        return copy(
            mixed.at[dc], summed_ref.at[:, :, part(other), :],
            send2.at[dc], recv2.at[dc], (other, slab),
        )

    def share(dc):
        piece = shares.at[column]
        return copy(piece, piece, send3.at[dc], recv3.at[dc], (partner(dc), slab))

    def share_in(dc):
        other = partner(-dc)
        piece = shares.at[other]
        return copy(piece, piece, send3.at[dc], recv3.at[dc], (other, slab))

    for r in span:
        for dc in others:
            outward_in(r, dc).wait_recv()
    for dc in others:
        mixed[dc] = mix(partner(dc))
        homeward(dc).start()

    levels = jnp.zeros((depth, size), F32)
    for e in range(count):
        energy = ENERGY_LOW + ENERGY_SPAN * e / count
        occupation = 1.0 / (1.0 + math.exp(3.0 * (energy - (ENERGY_LOW + 0.5 * ENERGY_SPAN))))
        levels = levels - occupation * taken[e, 1]
    local_rows, local_cols = iotas((depth, size))
    diagonal = jnp.where(local_rows + column * depth == local_cols, levels, 0.0)
    own_share = jnp.sum(diagonal, axis=0, keepdims=True)
    shares[column] = jnp.broadcast_to(own_share, (8, size))
    for dc in others:
        share(dc).start()

    summed_ref[:, :, part(column), :] = mix(column)
    for dc in others:
        share_in(dc).wait_recv()
    density_ref[...] = jnp.sum(shares[...], axis=0)[:1]
    for dc in others:
        homeward_in(dc).wait_recv()
    for target in range(slabs):
        @pl.when(slab != target)
        def _():
            along(target).wait_send()
            for dc in others:
                across(target, dc).wait_send()
    for dc in others:
        for r in span:
            outward(r, dc).wait_send()
        homeward(dc).wait_send()
        share(dc).wait_send()


def coupling_kernel(summed_ref, coupling_ref, green_in, out_ref, green_out, sem):
    through = pltpu.make_async_copy(green_in, green_out, sem)
    through.start()
    high, low = split(coupling_ref[...])
    left = jnp.concatenate([high, low, high], axis=1)
    for r in range(summed_ref.shape[0]):
        for part in range(2):
            a, b = split(summed_ref[r, part])
            out_ref[r, part] = dot(left, jnp.concatenate([a, a, b], axis=0))
    through.wait()


def whole():
    return pl.BlockSpec(memory_space=pltpu.VMEM)


def scalar():
    return pl.BlockSpec(memory_space=pltpu.SMEM)


def anywhere():
    return pl.BlockSpec(memory_space=pl.ANY)


def per_device(slabs, columns, hamiltonian, contact, hop, bond, shifts, strength, coupling):
    size = hamiltonian.shape[-1]
    row_count = contact.shape[0]
    depth = size // columns
    dma = pltpu.SemaphoreType.DMA
    block = jax.ShapeDtypeStruct((row_count, 2, size, size), F32)
    green, summed, density = pl.pallas_call(
        functools.partial(born_kernel, slabs, columns),
        out_shape=(block, block, jax.ShapeDtypeStruct((1, size), F32)),
        in_specs=[whole()] * 4 + [scalar()] * 2 + [whole()],
        out_specs=(whole(),) * 3,
        scratch_shapes=[
            pltpu.VMEM((slabs, size, size), F32),
            pltpu.VMEM((row_count * columns, 2, depth, size), F32),
            pltpu.VMEM((columns, row_count, 2, depth, size), F32),
            pltpu.VMEM((columns, 8, size), F32),
            dma((slabs,)), dma((slabs,)),
            dma((slabs, columns)), dma((slabs, columns)),
            dma((row_count, columns)), dma((row_count, columns)),
            dma((columns,)), dma((columns,)), dma((columns,)), dma((columns,)),
        ],
        compiler_params=pltpu.CompilerParams(
            collective_id=0, has_side_effects=True, vmem_limit_bytes=VMEM_LIMIT
        ),
        name="born",
    )(hamiltonian[0], contact[:, 0], hop, bond, shifts, strength, coupling)
    self_energy, green = pl.pallas_call(
        coupling_kernel,
        out_shape=(block, block),
        in_specs=[whole(), whole(), anywhere()],
        out_specs=(whole(), anywhere()),
        scratch_shapes=[dma],
        compiler_params=pltpu.CompilerParams(vmem_limit_bytes=VMEM_LIMIT),
        name="coupling",
    )(summed, coupling, green)
    return (green[:, None, None], self_energy[:, None, None], density)


def solution(mesh):
    in_specs = (
        P("slab", None, None, None),
        P(None, "energy", None, None, None, None),
        P(),
        P(),
        P(),
        P(),
        P(),
    )
    out_specs = (
        P(None, "energy", "slab", None, None, None),
        P(None, "energy", "slab", None, None, None),
        P("slab", None),
    )
    return jax.shard_map(
        functools.partial(per_device, mesh.shape["slab"], mesh.shape["energy"]),
        mesh=mesh, in_specs=in_specs, out_specs=out_specs, check_vma=False,
    )
```

time: 75.4 us -> 96.3 us (1.28)
  Pallas kernels: 73.9 us -> 94.9 us
    pallas_call x4 -> x2, Pallas kernels: 73.9 us -> 94.9 us  [the longest x1 59.8 us: per_device(): pl.pallas_call(functools.partial(born_kernel, slabs, columns), out_shape=...]
where the time goes in v1:
time: 96.3 us; the launch traced here: 96.1 us
  Pallas kernels  94.9 us (99%)
    pallas_call x1, Pallas kernels, per_device(): pl.pallas_call(functools.partial(born_kernel, slabs, columns), out_shape=...  59.8 us
    pallas_call x1, Pallas kernels, per_device(): pl.pallas_call(coupling_kernel, out_shape=(block, block), in_specs=[whole...  35.1 us

profile of v1, /device:TPU:0, one launch (start us, length us, event | category | flops | bytes accessed | tf_op | source)
XLA Modules:
  0.0 96.1 jit_solution(11265310608144656349)
XLA Ops:
  0.6 59.8 %born.1 = (f32[2,2,256,256]{3,2,1,0:T(8,128)}, f32[2,2,256,256]{3,2,1,0:T(8,128)}, f32[1,256]{1,0:T(1,128)}) custom-call(f32[2,256,256]{2,1,0:T(8,128)} %bitcast.9, f32[2,2,2,256,256]{4,3,2,1,0:T(8,128)} %bitcast.8, f32[3,256]{1,0:T(4,128)} %hop_ref.1, s32[3,256]{1,0:T(4,128)} %bond_ref.1, s32[4]{0:T(128)} %shifts_ref.1, f32[4]{0:T(128)} %strength_ref.1, ...), custom_call_target="tpu_custom_call" | custom-call | tf_op jit(solution)/shard_map/born/pallas_call | solution.py:367
  60.4 0.0 copy-start
  60.5 35.1 %coupling.1 = (f32[2,2,256,256]{3,2,1,0:T(8,128)}, f32[2,2,256,256]{3,2,1,0:T(8,128)}) custom-call(f32[2,2,256,256]{3,2,1,0:T(8,128)} %get-tuple-element.8.summed_ref, f32[256,256]{1,0:T(8,128)} %coupling_ref.3, f32[2,2,256,256]{3,2,1,0:T(8,128)} %get-tuple-element.9.green_in), custom_call_target="tpu_custom_call" | custom-call | tf_op jit(solution)/shard_map/coupling/pallas_call | solution.py:387
  95.6 0.0 copy-done
  95.6 0.6 copy.13
Async XLA Ops:
  60.4 35.1 %copy-start = (f32[1,256]{1,0:T(1,128)S(1)}, f32[1,256]{1,0:T(1,128)}, u32[]{:S(2)}) copy-start(f32[1,256]{1,0:T(1,128)} %get-tuple-element.21) | copy-start | bytes 3076

commit v2 on v1

--- a/solution.py
+++ b/solution.py
@@ -40,10 +40,18 @@
     ai, am = split(a[1])
     br, bl = split(b[0])
     bi, bm = split(b[1])
-    left = jnp.concatenate([ar, al, ar, ai, am, ai], axis=1)
-    real = jnp.concatenate([br, br, bl, -bi, -bi, -bm], axis=0)
-    imag = jnp.concatenate([bi, bi, bm, br, br, bl], axis=0)
-    return dot(left, real), dot(left, imag)
+    left = jnp.concatenate(
+        [jnp.concatenate([ar, ai], axis=1), jnp.concatenate([al, am], axis=1)], axis=0
+    )
+    high = jnp.concatenate(
+        [jnp.concatenate([br, bi], axis=1), jnp.concatenate([-bi, br], axis=1)], axis=0
+    )
+    low = jnp.concatenate(
+        [jnp.concatenate([bl, bm], axis=1), jnp.concatenate([-bm, bl], axis=1)], axis=0
+    )
+    full = dot(left, high)
+    both = full[:size] + (full[size:] + dot(left[:size], low))
+    return both[:, :size], both[:, size:]
 
 
 def invert(x):
@@ -81,8 +89,8 @@
 
 
 def born_kernel(
-    slabs, columns, ham_ref, contact_ref, hop_ref, bond_ref, shifts_ref, strength_ref,
-    coupling_ref, green_ref, summed_ref, density_ref, hall, taken, mixed, shares,
+    slabs, columns, ham_ref, contact_hbm, hop_ref, bond_ref, shifts_ref, strength_ref,
+    coupling_ref, green_ref, summed_ref, density_ref, contact_ref, contact_sem, hall, taken, mixed, shares,
     send_z, recv_z, send_h, recv_h, send1, recv1, send2, recv2, send3, recv3,
 ):
     column = lax.axis_index("energy")
@@ -111,6 +119,9 @@
             device_id=device, device_id_type=MESH,
         )
 
+    fetch = pltpu.make_async_copy(contact_hbm, contact_ref, contact_sem)
+    fetch.start()
+
     barrier = pltpu.get_barrier_semaphore()
     for dz in range(1, slabs):
         pl.semaphore_signal(
@@ -207,6 +218,7 @@
         ]
 
     is_right = jnp.logical_not(is_left)
+    fetch.wait()
     arrive(0, is_left)
     arrive(last, is_right)
     near = end_inverses(choose(0, last), choose(0, 1))
@@ -334,9 +346,12 @@
         share(dc).wait_send()
 
 
-def coupling_kernel(summed_ref, coupling_ref, green_in, out_ref, green_out, sem):
+def coupling_kernel(
+    summed_ref, coupling_ref, density_in, green_in, out_ref, density_out, green_out, sem
+):
     through = pltpu.make_async_copy(green_in, green_out, sem)
     through.start()
+    density_out[...] = density_in[...]
     high, low = split(coupling_ref[...])
     left = jnp.concatenate([high, low, high], axis=1)
     for r in range(summed_ref.shape[0]):
@@ -367,9 +382,11 @@
     green, summed, density = pl.pallas_call(
         functools.partial(born_kernel, slabs, columns),
         out_shape=(block, block, jax.ShapeDtypeStruct((1, size), F32)),
-        in_specs=[whole()] * 4 + [scalar()] * 2 + [whole()],
+        in_specs=[whole(), anywhere(), whole(), whole(), scalar(), scalar(), whole()],
         out_specs=(whole(),) * 3,
         scratch_shapes=[
+            pltpu.VMEM((row_count, 2, 2, size, size), F32),
+            dma,
             pltpu.VMEM((slabs, size, size), F32),
             pltpu.VMEM((row_count * columns, 2, depth, size), F32),
             pltpu.VMEM((columns, row_count, 2, depth, size), F32),
@@ -384,15 +401,15 @@
         ),
         name="born",
     )(hamiltonian[0], contact[:, 0], hop, bond, shifts, strength, coupling)
-    self_energy, green = pl.pallas_call(
+    self_energy, density, green = pl.pallas_call(
         coupling_kernel,
-        out_shape=(block, block),
-        in_specs=[whole(), whole(), anywhere()],
-        out_specs=(whole(), anywhere()),
+        out_shape=(block, jax.ShapeDtypeStruct((1, size), F32), block),
+        in_specs=[whole()] * 4,
+        out_specs=(whole(), whole(), anywhere()),
         scratch_shapes=[dma],
         compiler_params=pltpu.CompilerParams(vmem_limit_bytes=VMEM_LIMIT),
         name="coupling",
-    )(summed, coupling, green)
+    )(summed, coupling, density, green)
     return (green[:, None, None], self_energy[:, None, None], density)
 
 

time: 96.3 us -> 63.6 us (0.66)
  Pallas kernels: 94.9 us -> 62.6 us
    pallas_call x1, Pallas kernels: 35.1 us -> 3.59 us  [per_device(): pl.pallas_call(coupling_kernel, out_shape=(block, jax.ShapeDtypeStruct((1...]
where the time goes in v2:
time: 63.6 us; the launch traced here: 63.4 us
  Pallas kernels  62.6 us (98%)
  between operations  0.8 us (1%)
    pallas_call x1, Pallas kernels, per_device(): pl.pallas_call(functools.partial(born_kernel, slabs, columns), out_shape=...  59 us
    pallas_call x1, Pallas kernels, per_device(): pl.pallas_call(coupling_kernel, out_shape=(block, jax.ShapeDtypeStruct((1...  3.59 us

profile of v2, /device:TPU:0, one launch (start us, length us, event | category | flops | bytes accessed | tf_op | source)
XLA Modules:
  0.0 63.4 jit_solution(9574827335591506158)
XLA Ops:
  0.6 59.0 %born.1 = (f32[2,2,256,256]{3,2,1,0:T(8,128)}, f32[2,2,256,256]{3,2,1,0:T(8,128)}, f32[1,256]{1,0:T(1,128)}) custom-call(f32[2,256,256]{2,1,0:T(8,128)} %bitcast.9, f32[2,2,2,256,256]{4,3,2,1,0:T(8,128)} %bitcast.8, f32[3,256]{1,0:T(4,128)} %hop_ref.1, s32[3,256]{1,0:T(4,128)} %bond_ref.1, s32[4]{0:T(128)} %shifts_ref.1, f32[4]{0:T(128)} %strength_ref.1, ...), custom_call_target="tpu_custom_call" | custom-call | tf_op jit(solution)/shard_map/born/pallas_call | solution.py:382
  59.7 3.6 %coupling.1 = (f32[2,2,256,256]{3,2,1,0:T(8,128)}, f32[1,256]{1,0:T(1,128)}, f32[2,2,256,256]{3,2,1,0:T(8,128)}) custom-call(f32[2,2,256,256]{3,2,1,0:T(8,128)} %get-tuple-element.9.summed_ref, f32[256,256]{1,0:T(8,128)} %coupling_ref.3, f32[1,256]{1,0:T(1,128)} %get-tuple-element.10.density_in, f32[2,2,256,256]{3,2,1,0:T(8,128)} %get-tuple-element.11.green_in), custom_call_target="tpu_custom_call" | custom-call | tf_op jit(solution)/shard_map/coupling/pallas_call | solution.py:404

commit v3 on v2

--- a/solution.py
+++ b/solution.py
@@ -66,13 +66,13 @@
         modulus = dr * dr + di * di
         recips.append((dr / modulus, -di / modulus))
     (cr, ci), (rr, ri) = recips
-    pr = x[0] * cr - x[1] * ci
-    pi = x[0] * ci + x[1] * cr
-    qr = jnp.where(eye, 2.0, 0.0) - pr
-    qi = -pi
-    first = (rr * qr - ri * qi, rr * qi + ri * qr)
-    yr, yi = product(x, first)
-    return product(first, (jnp.where(eye, 2.0, 0.0) - yr, -yi))
+    unit = jnp.where(eye, 1.0, 0.0)
+    w = (unit - (x[0] * cr - x[1] * ci), -(x[0] * ci + x[1] * cr))
+    v = product(w, w)
+    t = product(w, v)
+    sr = unit + (w[0] + (v[0] + t[0]))
+    si = w[1] + (v[1] + t[1])
+    return rr * sr - ri * si, rr * si + ri * sr
 
 
 def conjugate(x, coupler):
@@ -224,7 +224,7 @@
     near = end_inverses(choose(0, last), choose(0, 1))
     arrive(0, is_right)
     arrive(last, is_left)
-    far = end_inverses(choose(last, 0), choose(1, 0))
+    far_ham, far_end = onsite(choose(last, 0)), choose(1, 0)
     for source in range(1, last):
         arrive(source, slab >= 0)
     mid_ham = onsite(choose(half - 1, half))
@@ -243,24 +243,6 @@
             green_ref.at[r, :, part(other), :], taken.at[r * columns + other],
             send1.at[r, dc], recv1.at[r, dc], (other, slab),
         )
-
-    for r in span:
-        opposite = invert(minus(base(r, cross_ham), conjugate(far[r], far_side)))
-        reduced = minus(base(r, mid_ham), conjugate(near[r], near_side))
-        middle = invert(minus(reduced, conjugate(opposite, cross_side)))
-        green_ref[r, 0] = middle[0]
-        green_ref[r, 1] = middle[1]
-
-        @pl.when(jnp.logical_or(slab == 0, slab == last))
-        def _():
-            inner = conjugate((green_ref[r, 0], green_ref[r, 1]), near_back)
-            change = product(product(near[r], inner), near[r])
-            green_ref[r, 0] = near[r][0] + change[0]
-            green_ref[r, 1] = near[r][1] + change[1]
-
-        for dc in others:
-            outward(r, dc).start()
-        taken[r * columns + column] = green_ref[r, :, part(column), :]
 
     weights = {}
     for d in range(-KMAX, KMAX + 1):
@@ -272,32 +254,41 @@
     high, low = split(coupling_ref[...].T)
     right = jnp.concatenate([high, high, low], axis=0)
 
-    def mix(target):
-        pieces = []
-        for r in span:
-            place = r * columns + target
-            total = jnp.zeros((2, depth, size), F32)
-            for d, weight in weights.items():
-                inside = jnp.logical_and(place + d >= 0, place + d < count)
-                index = jnp.clip(place + d, 0, count - 1)
-                total = total + jnp.where(inside, weight, 0.0) * taken[index]
-            pieces.append(total.reshape(2 * depth, size))
-        a, b = split(jnp.concatenate(pieces, axis=0))
+    def mix(r, target):
+        place = r * columns + target
+        total = jnp.zeros((2, depth, size), F32)
+        for d, weight in weights.items():
+            inside = jnp.logical_and(place + d >= 0, place + d < count)
+            index = jnp.clip(place + d, 0, count - 1)
+            total = total + jnp.where(inside, weight, 0.0) * taken[index]
+        a, b = split(total.reshape(2 * depth, size))
         moved = dot(jnp.concatenate([a, b, a], axis=1), right)
-        return moved.reshape(row_count, 2, depth, size)
-
-    def homeward(dc):
+        return moved.reshape(2, depth, size)
+
+    def homeward(r, dc):
         return copy(
-            mixed.at[dc], summed_ref.at[:, :, part(column), :],
-            send2.at[dc], recv2.at[dc], (partner(dc), slab),
-        )
-
-    def homeward_in(dc):
+            mixed.at[dc, r], summed_ref.at[r, :, part(column), :],
+            send2.at[r, dc], recv2.at[r, dc], (partner(dc), slab),
+        )
+
+    def homeward_in(r, dc):
         other = partner(-dc)
         return copy(
-            mixed.at[dc], summed_ref.at[:, :, part(other), :],
-            send2.at[dc], recv2.at[dc], (other, slab),
-        )
+            mixed.at[dc, r], summed_ref.at[r, :, part(other), :],
+            send2.at[r, dc], recv2.at[r, dc], (other, slab),
+        )
+
+    def send_home(r, dc):
+        mixed[dc, r] = mix(r, partner(dc))
+        homeward(r, dc).start()
+
+    def settle(r):
+        for dc in others:
+            outward_in(r, dc).wait_recv()
+        for dc in others:
+            @pl.when(partner(dc) < columns - KMAX)
+            def _():
+                send_home(r, dc)
 
     def share(dc):
         piece = shares.at[column]
@@ -309,11 +300,36 @@
         return copy(piece, piece, send3.at[dc], recv3.at[dc], (other, slab))
 
     for r in span:
+        far = invert(
+            minus(base(r, far_ham), (contact_ref[r, far_end, 0], contact_ref[r, far_end, 1]))
+        )
+        opposite = invert(minus(base(r, cross_ham), conjugate(far, far_side)))
+        reduced = minus(base(r, mid_ham), conjugate(near[r], near_side))
+        if r > 0:
+            settle(r - 1)
+        middle = invert(minus(reduced, conjugate(opposite, cross_side)))
+        green_ref[r, 0] = middle[0]
+        green_ref[r, 1] = middle[1]
+
+        @pl.when(jnp.logical_or(slab == 0, slab == last))
+        def _():
+            inner = conjugate((green_ref[r, 0], green_ref[r, 1]), near_back)
+            change = product(product(near[r], inner), near[r])
+            green_ref[r, 0] = near[r][0] + change[0]
+            green_ref[r, 1] = near[r][1] + change[1]
+
         for dc in others:
-            outward_in(r, dc).wait_recv()
-    for dc in others:
-        mixed[dc] = mix(partner(dc))
-        homeward(dc).start()
+            outward(r, dc).start()
+        taken[r * columns + column] = green_ref[r, :, part(column), :]
+
+    for dc in others:
+        outward_in(row_count - 1, dc).wait_recv()
+    for dc in others:
+        send_home(row_count - 1, dc)
+        for r in range(row_count - 1):
+            @pl.when(partner(dc) >= columns - KMAX)
+            def _():
+                send_home(r, dc)
 
     levels = jnp.zeros((depth, size), F32)
     for e in range(count):
@@ -327,12 +343,14 @@
     for dc in others:
         share(dc).start()
 
-    summed_ref[:, :, part(column), :] = mix(column)
+    for r in span:
+        summed_ref[r, :, part(column), :] = mix(r, column)
     for dc in others:
         share_in(dc).wait_recv()
     density_ref[...] = jnp.sum(shares[...], axis=0)[:1]
     for dc in others:
-        homeward_in(dc).wait_recv()
+        for r in span:
+            homeward_in(r, dc).wait_recv()
     for target in range(slabs):
         @pl.when(slab != target)
         def _():
@@ -342,7 +360,7 @@
     for dc in others:
         for r in span:
             outward(r, dc).wait_send()
-        homeward(dc).wait_send()
+            homeward(r, dc).wait_send()
         share(dc).wait_send()
 
 
@@ -394,7 +412,8 @@
             dma((slabs,)), dma((slabs,)),
             dma((slabs, columns)), dma((slabs, columns)),
             dma((row_count, columns)), dma((row_count, columns)),
-            dma((columns,)), dma((columns,)), dma((columns,)), dma((columns,)),
+            dma((row_count, columns)), dma((row_count, columns)),
+            dma((columns,)), dma((columns,)),
         ],
         compiler_params=pltpu.CompilerParams(
             collective_id=0, has_side_effects=True, vmem_limit_bytes=VMEM_LIMIT

time: 63.6 us -> 66 us (1.038)
  the two profiles are of different devices: /device:TPU:0 before, /device:TPU:7 now
where the time goes in v3:
time: 66 us; the launch traced here: 65.9 us
  Pallas kernels  65.1 us (99%)
  between operations  0.8 us (1%)
    pallas_call x1, Pallas kernels, per_device(): pl.pallas_call(functools.partial(born_kernel, slabs, columns), out_shape=...  61.5 us
    pallas_call x1, Pallas kernels, per_device(): pl.pallas_call(coupling_kernel, out_shape=(block, jax.ShapeDtypeStruct((1...  3.59 us

profile of v3, /device:TPU:7, one launch (start us, length us, event | category | flops | bytes accessed | tf_op | source)
XLA Modules:
  0.0 65.9 jit_solution(17926854744393983011)
XLA Ops:
  0.6 61.5 %born.1 = (f32[2,2,256,256]{3,2,1,0:T(8,128)}, f32[2,2,256,256]{3,2,1,0:T(8,128)}, f32[1,256]{1,0:T(1,128)}) custom-call(f32[2,256,256]{2,1,0:T(8,128)} %bitcast.9, f32[2,2,2,256,256]{4,3,2,1,0:T(8,128)} %bitcast.8, f32[3,256]{1,0:T(4,128)} %hop_ref.1, s32[3,256]{1,0:T(4,128)} %bond_ref.1, s32[4]{0:T(128)} %shifts_ref.1, f32[4]{0:T(128)} %strength_ref.1, ...), custom_call_target="tpu_custom_call" | custom-call | tf_op jit(solution)/shard_map/born/pallas_call | solution.py:400
  62.1 3.6 %coupling.1 = (f32[2,2,256,256]{3,2,1,0:T(8,128)}, f32[1,256]{1,0:T(1,128)}, f32[2,2,256,256]{3,2,1,0:T(8,128)}) custom-call(f32[2,2,256,256]{3,2,1,0:T(8,128)} %get-tuple-element.9.summed_ref, f32[256,256]{1,0:T(8,128)} %coupling_ref.3, f32[1,256]{1,0:T(1,128)} %get-tuple-element.10.density_in, f32[2,2,256,256]{3,2,1,0:T(8,128)} %get-tuple-element.11.green_in), custom_call_target="tpu_custom_call" | custom-call | tf_op jit(solution)/shard_map/coupling/pallas_call | solution.py:423

commit v4 on v2

--- a/solution.py
+++ b/solution.py
@@ -66,13 +66,13 @@
         modulus = dr * dr + di * di
         recips.append((dr / modulus, -di / modulus))
     (cr, ci), (rr, ri) = recips
-    pr = x[0] * cr - x[1] * ci
-    pi = x[0] * ci + x[1] * cr
-    qr = jnp.where(eye, 2.0, 0.0) - pr
-    qi = -pi
-    first = (rr * qr - ri * qi, rr * qi + ri * qr)
-    yr, yi = product(x, first)
-    return product(first, (jnp.where(eye, 2.0, 0.0) - yr, -yi))
+    unit = jnp.where(eye, 1.0, 0.0)
+    w = (unit - (x[0] * cr - x[1] * ci), -(x[0] * ci + x[1] * cr))
+    v = product(w, w)
+    t = product(w, v)
+    sr = unit + (w[0] + (v[0] + t[0]))
+    si = w[1] + (v[1] + t[1])
+    return rr * sr - ri * si, rr * si + ri * sr
 
 
 def conjugate(x, coupler):

time: 63.6 us -> 63.5 us (level)
  no operation moved by 1% of the time
where the time goes in v4:
time: 63.5 us; the launch traced here: 63.3 us
  Pallas kernels  62.5 us (98%)
  between operations  0.8 us (1%)
    pallas_call x1, Pallas kernels, per_device(): pl.pallas_call(functools.partial(born_kernel, slabs, columns), out_shape=...  58.9 us
    pallas_call x1, Pallas kernels, per_device(): pl.pallas_call(coupling_kernel, out_shape=(block, jax.ShapeDtypeStruct((1...  3.59 us

profile of v4, /device:TPU:0, one launch (start us, length us, event | category | flops | bytes accessed | tf_op | source)
XLA Modules:
  0.0 63.3 jit_solution(16065800813941717464)
XLA Ops:
  0.6 58.9 %born.1 = (f32[2,2,256,256]{3,2,1,0:T(8,128)}, f32[2,2,256,256]{3,2,1,0:T(8,128)}, f32[1,256]{1,0:T(1,128)}) custom-call(f32[2,256,256]{2,1,0:T(8,128)} %bitcast.9, f32[2,2,2,256,256]{4,3,2,1,0:T(8,128)} %bitcast.8, f32[3,256]{1,0:T(4,128)} %hop_ref.1, s32[3,256]{1,0:T(4,128)} %bond_ref.1, s32[4]{0:T(128)} %shifts_ref.1, f32[4]{0:T(128)} %strength_ref.1, ...), custom_call_target="tpu_custom_call" | custom-call | tf_op jit(solution)/shard_map/born/pallas_call | solution.py:382
  59.6 3.6 %coupling.1 = (f32[2,2,256,256]{3,2,1,0:T(8,128)}, f32[1,256]{1,0:T(1,128)}, f32[2,2,256,256]{3,2,1,0:T(8,128)}) custom-call(f32[2,2,256,256]{3,2,1,0:T(8,128)} %get-tuple-element.9.summed_ref, f32[256,256]{1,0:T(8,128)} %coupling_ref.3, f32[1,256]{1,0:T(1,128)} %get-tuple-element.10.density_in, f32[2,2,256,256]{3,2,1,0:T(8,128)} %get-tuple-element.11.green_in), custom_call_target="tpu_custom_call" | custom-call | tf_op jit(solution)/shard_map/coupling/pallas_call | solution.py:404
